TPU v7x, 512 devices: a whole 4x8x8 slice. The times are simulated.
512 devices in a mesh: dp: 32 (over z, x), ctx: 16 (over y, core).
Axes of the slice: x: 4, y: 8, z: 8, core: 2. Of those that a mesh axis runs over, the one named last changes fastest.
Arguments:
- query: bfloat16 [64, 1024, 4096], P('dp', 'ctx'), may hold values from -6 to 6
- key_in: bfloat16 [64, 1024, 1024], P('dp', 'ctx'), may hold values from -6 to 6
- value_in: bfloat16 [64, 1024, 1024], P('dp', 'ctx'), may hold values from -6 to 6
- out_grad: bfloat16 [64, 1024, 4096], P('dp', 'ctx'), may hold values from -1.5 to 1.5
- masked: int32 [64, 512], P('dp'), may hold values from 0 to 1023, as said below
- bucket: int32 [64, 1024], P('dp', 'ctx'), may hold values from 0 to 15
Outputs:
- query_grad: bfloat16 [64, 1024, 4096], P('dp', 'ctx')
- key_grad: bfloat16 [64, 1024, 1024], P('dp', 'ctx')
- value_grad: bfloat16 [64, 1024, 1024], P('dp', 'ctx')
- bias_query_grad: float32 [16, 256], P('ctx', 'dp')
- bias_kv_grad: float32 [2, 1024], P(None, 'dp')
Inputs may be any that keep to these rules, and one draw needn't show every extreme that they name: Each document has exactly 512 distinct masked positions.
All inputs are finite; a program needn't handle non-finite values.
Results may differ from a plain program's by a relative error of at most 0.012.
The roundings to bfloat16 on the way count: a program that leaves them out, or rounds other values in their place, can miss the bound.
Values may be sent and summed in bfloat16 or wider, within the bound.
A program may use at most 64 MiB of HBM per device.

v0:
```python
import math

import jax
import jax.numpy as jnp
from jax import lax
from jax.sharding import PartitionSpec as P

H = 32
KVH = 8
HD = 128
NB = 16


def in_one_piece(arrays, axis, split_dim, concat_dim, along):
    widths = [a.shape[along] for a in arrays]
    both = jnp.concatenate(arrays, axis=along)
    filled = lax.all_to_all(both, axis, split_axis=split_dim, concat_axis=concat_dim, tiled=True)
    return tuple(jnp.split(filled, [sum(widths[:k]) for k in range(1, len(widths))], axis=along))


def sent_to_all(value, axis):
    length = lax.axis_size(axis)
    return lax.all_to_all(
        jnp.broadcast_to(value[None], (length, *value.shape)), axis, 0, 0, tiled=True
    )


def of_everyone(value, axis):
    everything = sent_to_all(value, axis)
    return jnp.sum(everything, axis=0)


def in_one(arrays, axis):
    line, at, finished = (jnp.concatenate([a.reshape(-1) for a in arrays]), 0, [])
    so_far = of_everyone(line, axis)
    for a in arrays:
        finished.append(so_far[at : at + a.size].reshape(a.shape))
        at += a.size
    return tuple(finished)


def softmax_rows(scores):
    shifted = scores - jnp.max(scores, axis=-1, keepdims=True)
    exponent = jnp.exp(shifted)
    return exponent / jnp.sum(exponent, axis=-1, keepdims=True)


def head_pass(inputs):
    query_one, key_one, value_one, cot_one = inputs
    inv_root = 1.0 / math.sqrt(HD)
    scores = (
        jnp.einsum("qd,kd->qk", query_one, key_one, preferred_element_type=jnp.float32) * inv_root
    )
    attn_probs = softmax_rows(scores)
    probs_low = attn_probs.astype(jnp.bfloat16)
    attn_out = jnp.einsum("qk,kd->qd", probs_low, value_one, preferred_element_type=jnp.float32)
    delta_rows = jnp.sum(cot_one.astype(jnp.float32) * attn_out, axis=-1)
    value_full = jnp.einsum("qk,qd->kd", probs_low, cot_one, preferred_element_type=jnp.float32)
    prob_grad = jnp.einsum("qd,kd->qk", cot_one, value_one, preferred_element_type=jnp.float32)
    score_low = (attn_probs * (prob_grad - delta_rows[:, None]) * inv_root).astype(jnp.bfloat16)
    query_full = jnp.einsum("qk,kd->qd", score_low, key_one, preferred_element_type=jnp.float32)
    key_full = jnp.einsum("qk,qd->kd", score_low, query_one, preferred_element_type=jnp.float32)
    return (query_full, key_full, value_full)


def to_items(array, count):
    docs_here, length = (array.shape[0], array.shape[1])
    return (
        array.reshape(docs_here, length, count, HD)
        .transpose(0, 2, 1, 3)
        .reshape(docs_here * count, length, HD)
    )


def attend_heads(query_here, key_here, value_here, cot_here, heads_dev, slots_dev):
    docs_here, length = (query_here.shape[0], query_here.shape[1])
    per_slot = heads_dev // slots_dev

    def widen(array):
        shaped = array.reshape(docs_here, length, slots_dev, HD).transpose(0, 2, 1, 3)
        return jnp.repeat(shaped, per_slot, axis=1).reshape(docs_here * heads_dev, length, HD)

    query_full, key_full, value_full = lax.map(
        head_pass,
        (
            to_items(query_here, heads_dev),
            widen(key_here),
            widen(value_here),
            to_items(cot_here, heads_dev),
        ),
    )
    query_sums = jnp.sum(jnp.sum(query_full, axis=1).reshape(docs_here, heads_dev * HD), axis=0)
    query_back = query_full.astype(jnp.bfloat16).reshape(docs_here, heads_dev, length, HD)
    query_back = query_back.transpose(0, 2, 1, 3).reshape(docs_here, length, heads_dev * HD)

    def slot_rows(grads):
        merged = jnp.sum(grads.reshape(docs_here, slots_dev, per_slot, length, HD), axis=2)
        return merged.transpose(0, 2, 1, 3).reshape(docs_here, length, slots_dev * HD)

    return (query_back, slot_rows(key_full), slot_rows(value_full), query_sums)


def per_device(query, key_in, value_in, out_grad, masked, bucket):
    n_ctx = lax.axis_size("ctx")
    n_dp = lax.axis_size("dp")
    docs_dev, tok_count = (query.shape[0], query.shape[1])
    length = tok_count * n_ctx
    heads_dev = H // n_ctx
    positions = lax.axis_index("ctx") * tok_count + jnp.arange(tok_count, dtype=jnp.int32)
    is_masked = jnp.any(masked[:, None, :] == positions[None, :, None], axis=-1)
    loss_weight = is_masked.astype(jnp.float32) * NB / (bucket.astype(jnp.float32) + 1.0)
    cotangent = (out_grad.astype(jnp.float32) * loss_weight[:, :, None]).astype(jnp.bfloat16)
    key_heads = key_in.reshape(docs_dev, tok_count, KVH, HD)
    value_heads = value_in.reshape(docs_dev, tok_count, KVH, HD)
    slot_total = max(KVH, n_ctx)
    copies = slot_total // KVH
    key_copies = jnp.repeat(key_heads, copies, axis=2).reshape(docs_dev, tok_count, slot_total * HD)
    value_copies = jnp.repeat(value_heads, copies, axis=2).reshape(
        docs_dev, tok_count, slot_total * HD
    )
    query_here, cot_here, key_here, value_here = (
        *in_one_piece((query, cotangent), "ctx", 2, 1, 0),
        *in_one_piece((key_copies, value_copies), "ctx", 2, 1, 0),
    )
    query_back, key_terms, value_terms, query_sums = attend_heads(
        query_here, key_here, value_here, cot_here, heads_dev, slot_total // n_ctx
    )
    key_rows, value_rows = tuple(
        (
            part.astype(jnp.float32)
            for part in in_one_piece(
                (key_terms.astype(jnp.bfloat16), value_terms.astype(jnp.bfloat16)), "ctx", 1, 2, 0
            )
        )
    )
    query_grad = lax.all_to_all(query_back, "ctx", split_axis=1, concat_axis=2, tiled=True)
    key_full = jnp.sum(key_rows.reshape(docs_dev, tok_count, KVH, copies, HD), axis=3).reshape(
        docs_dev, tok_count, KVH * HD
    )
    value_full = jnp.sum(value_rows.reshape(docs_dev, tok_count, KVH, copies, HD), axis=3).reshape(
        docs_dev, tok_count, KVH * HD
    )
    pair_local = jnp.stack([jnp.sum(key_full, axis=(0, 1)), jnp.sum(value_full, axis=(0, 1))])
    pair_group = of_everyone(pair_local, "ctx")
    query_total, pair_total = in_one((query_sums, pair_group), "dp")
    norm_factor = 1.0 / math.sqrt(docs_dev * n_dp * length)
    dp_index = lax.axis_index("dp")
    query_width = query_total.shape[0] // n_dp
    pair_width = pair_total.shape[1] // n_dp
    query_piece = lax.dynamic_slice_in_dim(query_total, dp_index * query_width, query_width, 0)
    pair_piece = lax.dynamic_slice_in_dim(pair_total, dp_index * pair_width, pair_width, 1)
    return (
        query_grad,
        key_full.astype(jnp.bfloat16),
        value_full.astype(jnp.bfloat16),
        (query_piece * norm_factor).reshape(1, query_width),
        pair_piece * norm_factor,
    )


def solution(mesh):
    in_specs = (
        P("dp", "ctx", None),
        P("dp", "ctx", None),
        P("dp", "ctx", None),
        P("dp", "ctx", None),
        P("dp", None),
        P("dp", "ctx"),
    )
    out_specs = (
        P("dp", "ctx", None),
        P("dp", "ctx", None),
        P("dp", "ctx", None),
        P("ctx", "dp"),
        P(None, "dp"),
    )
    return jax.shard_map(
        per_device, mesh=mesh, in_specs=in_specs, out_specs=out_specs, check_vma=False
    )
```

profile of v0, /device:TPU:1, one launch (start us, length us, event | category | flops | bytes accessed | tf_op | source)
XLA Modules:
  0.0 262.7 jit_solution(16353148668708557992)
XLA Ops:
  0.6 1.3 copy.138
  1.9 1.3 copy.139
  4.8 2.8 %fusion.36 = bf16[2048,4,64]{2,1,0:T(4,128)(2,1)S(1)} fusion(bf16[2,64,2048]{1,0,2:T(2,128)(2,1)S(1)} %bitcast.142, bf16[2,64,2048]{1,0,2:T(2,128)(2,1)S(1)} %bitcast.141), kind=kLoop, calls=%fused_computation.59 | loop fusion | flops 2097152 | bytes 2097152
  7.6 2.2 reshape.120
  9.8 10.3 %all-to-all-start.1 = ((bf16[16,2,16384]{2,1,0:T(2,128)(2,1)}), bf16[16,2,16384]{2,1,0:T(2,128)(2,1)S(1)}, u32[]{:S(2)}, u32[]{:S(2)}) async-start(bf16[16,2,16384]{2,1,0:T(2,128)(2,1)} %reshape.120), calls=%async_computation.1 | async-start | bytes 2097152 | tf_op jit(solution)/shard_map/all_to_all | solution.py:17
  21.6 4.7 %copy.116 = bf16[4,64,4096]{1,0,2:T(4,128)(2,1)} copy(bf16[4,64,4096]{2,1,0:T(8,128)(2,1)S(1)} %pad_maximum_fusion) | data formatting | bytes 4194304 | tf_op jit(solution)/shard_map/concatenate | solution.py:16
  26.3 7.5 %reshape.118 = bf16[16,2,32768]{2,1,0:T(2,128)(2,1)} reshape(bf16[4096,4,64]{2,1,0:T(4,128)(2,1)} %bitcast.128) | data formatting | bytes 4194304
  33.9 14.3 %all-to-all-done.1 = bf16[16,2,16384]{2,1,0:T(2,128)(2,1)S(1)} async-done(((bf16[16,2,16384]{2,1,0:T(2,128)(2,1)}), bf16[16,2,16384]{2,1,0:T(2,128)(2,1)S(1)}, u32[]{:S(2)}, u32[]{:S(2)}) %all-to-all-start.1) | async-done | bytes 1048608 | tf_op jit(solution)/shard_map/all_to_all | solution.py:17
  48.1 3.8 %all-to-all-start = ((bf16[16,2,32768]{2,1,0:T(2,128)(2,1)}), bf16[16,2,32768]{2,1,0:T(2,128)(2,1)S(1)}, u32[]{:S(2)}, u32[]{:S(2)}) async-start(bf16[16,2,32768]{2,1,0:T(2,128)(2,1)} %reshape.118), calls=%async_computation | async-start | bytes 4194304 | tf_op jit(solution)/shard_map/all_to_all | solution.py:17
  52.0 2.4 reshape.121
  54.4 2.7 %copy.140 = bf16[4,64,16,128]{3,2,1,0:T(8,128)(2,1)S(1)} copy(bf16[4,64,16,128]{1,0,3,2:T(4,128)(2,1)} %bitcast.135) | data formatting | bytes 2097152 | tf_op jit(solution)/shard_map/all_to_all | solution.py:17
  59.2 41.4 %all-to-all-done = bf16[16,2,32768]{2,1,0:T(2,128)(2,1)S(1)} async-done(((bf16[16,2,32768]{2,1,0:T(2,128)(2,1)}), bf16[16,2,32768]{2,1,0:T(2,128)(2,1)S(1)}, u32[]{:S(2)}, u32[]{:S(2)}) %all-to-all-start) | async-done | bytes 2097184 | tf_op jit(solution)/shard_map/all_to_all | solution.py:17
  100.6 5.0 %reshape.119 = bf16[4096,4,64]{2,1,0:T(4,128)(2,1)} reshape(bf16[16,2,32768]{2,1,0:T(2,128)(2,1)S(1)} %all-to-all-done) | data formatting | bytes 4194304
  105.6 5.6 %copy.117 = bf16[4,64,16,256]{3,1,2,0:T(8,128)(2,1)S(1)} copy(bf16[4,64,16,256]{1,0,3,2:T(4,128)(2,1)} %bitcast.129) | data formatting | bytes 4194304 | tf_op jit(solution)/shard_map/all_to_all | solution.py:17
  111.2 1.2 fusion.34
  112.4 1.3 reshape.104
  114.2 2.0 copy.141
  116.3 1.1 broadcast_in_dim.43
  117.5 36.6 %while.14 = (s32[]{:T(128)}, f32[4,1024,128]{2,1,0:T(8,128)}, f32[4,1024,128]{2,1,0:T(8,128)}, f32[4,1024,128]{2,1,0:T(8,128)}, bf16[4,1024,128]{2,1,0:T(8,128)(...) while((s32[]{:T(128)}, f32[4,1024,128]{2,1,0:T(8,128)}, ...), condition=%wide.region_5.6_spmd, body=%wide.region_1.5_spmd.sunk | while | flops 1631974400 | bytes 39635092 | solution.py:83
  119.4 1.8 fusion.68
  122.2 1.3 multiply_convert_fusion.3
  123.5 1.5 fusion.67
  125.1 1.5 fusion.66
  128.6 1.8 fusion.68
  131.4 1.3 multiply_convert_fusion.3
  132.7 1.5 fusion.67
  134.3 1.6 fusion.66
  137.8 1.7 fusion.68
  140.5 1.3 multiply_convert_fusion.3
  141.9 1.5 fusion.67
  143.4 1.6 fusion.66
  146.9 1.7 fusion.68
  148.6 1.0 fusion.65
  149.6 1.3 multiply_convert_fusion.3
  151.0 1.5 fusion.67
  152.5 1.6 fusion.66
  154.0 2.7 %bitcast_reduce_fusion = (bf16[2,1024,128]{2,1,0:T(8,128)(2,1)S(1)}, bf16[2,1024,128]{2,1,0:T(8,128)(2,1)S(1)}) fusion(f32[4,1024,128]{2,1,0:T(8,128)} %get-tuple-element.51, f32[4,1024,128]{2,1,0:T(8,128)} %get-tuple-element.50), kind=kLoop, calls=%fused_computation.40 | loop fusion | flops 524288 | bytes 5242880 | tf_op jit(solution)/shard_map/reduce_sum | solution.py:97
  157.6 33.4 %all_to_all.74 = bf16[4,1024,128]{2,0,1:T(4,128)(2,1)S(1)} all-to-all(bf16[4,1024,128]{2,0,1:T(4,128)(2,1)S(1)} %copy.130), channel_id=1, replica_groups=mesh['dp'=32,'ctx'=16] {'ctx'}, dimensions={1} | all-to-all | bytes 2097152 | tf_op jit(solution)/shard_map/all_to_all | solution.py:17
  192.7 3.4 %all-to-all-start.4 = ((f32[16,2,1024]{2,1,0:T(2,128)}), f32[16,2,1024]{2,1,0:T(2,128)S(1)}, u32[]{:S(2)}, u32[]{:S(2)}) async-start(f32[16,2,1024]{2,1,0:T(2,128)} %broadcast_in_dim.44), calls=%async_computation.4 | async-start | bytes 262144 | tf_op jit(solution)/shard_map/all_to_all | solution.py:23
  196.2 2.4 fusion.33
  199.1 2.0 copy.127
  201.2 3.4 %all-to-all-done.4 = f32[16,2,1024]{2,1,0:T(2,128)S(1)} async-done(((f32[16,2,1024]{2,1,0:T(2,128)}), f32[16,2,1024]{2,1,0:T(2,128)S(1)}, u32[]{:S(2)}, u32[]{:S(2)}) %all-to-all-start.4) | async-done | bytes 131104 | tf_op jit(solution)/shard_map/all_to_all | solution.py:23
  204.6 3.6 %all-to-all-start.2 = ((bf16[2,1024,256]{2,0,1:T(2,128)(2,1)}), bf16[2,1024,256]{2,0,1:T(2,128)(2,1)S(1)}, u32[]{:S(2)}, u32[]{:S(2)}) async-start(bf16[2,1024,256]{2,0,1:T(2,128)(2,1)} %copy.127), calls=%async_computation.2 | async-start | bytes 2097152 | tf_op jit(solution)/shard_map/all_to_all | solution.py:136
  208.2 27.7 %all-to-all-done.2 = bf16[2,1024,256]{2,0,1:T(2,128)(2,1)S(1)} async-done(((bf16[2,1024,256]{2,0,1:T(2,128)(2,1)}), bf16[2,1024,256]{2,0,1:T(2,128)(2,1)S(1)}, u32[]{:S(2)}, u32[]{:S(2)}) %all-to-all-start.2) | async-done | bytes 1048608 | tf_op jit(solution)/shard_map/all_to_all | solution.py:136
  236.8 11.1 %all-to-all-start.5 = ((f32[32,1,2304]{2,1,0:T(1,128)}), f32[32,1,2304]{2,1,0:T(1,128)S(1)}, u32[]{:S(2)}, u32[]{:S(2)}) async-start(f32[32,1,2304]{2,1,0:T(1,128)} %broadcast_in_dim.45), calls=%async_computation.5 | async-start | bytes 589824 | tf_op jit(solution)/shard_map/all_to_all | solution.py:23
  248.0 1.4 bitcast_reduce_fusion.2
  251.5 1.1 copy.149
  252.6 8.6 %all-to-all-done.5 = f32[32,1,2304]{2,1,0:T(1,128)S(1)} async-done(((f32[32,1,2304]{2,1,0:T(1,128)}), f32[32,1,2304]{2,1,0:T(1,128)S(1)}, u32[]{:S(2)}, u32[]{:S(2)}) %all-to-all-start.5) | async-done | bytes 294944 | tf_op jit(solution)/shard_map/all_to_all | solution.py:23
  (80 shorter events, 24.2 us)
Async XLA Ops:
  7.6 12.6 %copy-start.6 = (s32[2,512]{1,0:T(2,128)S(1)}, s32[2,512]{1,0:T(2,128)}, u32[]{:S(2)}) copy-start(s32[2,512]{1,0:T(2,128)} %param.12) | copy-start | bytes 12292
  7.6 12.8 %copy-start.7 = (s32[2,64]{1,0:T(2,128)S(1)}, s32[2,64]{1,0:T(2,128)}, u32[]{:S(2)}) copy-start(s32[2,64]{1,0:T(2,128)} %param.13) | copy-start | bytes 1540
  7.6 12.8 %copy-start.4 = (bf16[2,64,4096]{2,1,0:T(8,128)(2,1)S(1)}, bf16[2,64,4096]{2,1,0:T(8,128)(2,1)}, u32[]{:S(2)}) copy-start(bf16[2,64,4096]{2,1,0:T(8,128)(2,1)} %param.11) | copy-start | bytes 3145732
  9.8 38.3 %all-to-all-start.1 = ((bf16[16,2,16384]{2,1,0:T(2,128)(2,1)}), bf16[16,2,16384]{2,1,0:T(2,128)(2,1)S(1)}, u32[]{:S(2)}, u32[]{:S(2)}) async-start(bf16[16,2,16384]{2,1,0:T(2,128)(2,1)} %reshape.120), calls=%async_computation.1 | async-start | bytes 2097152 | tf_op jit(solution)/shard_map/all_to_all | solution.py:17
  20.2 1.2 copy-start.5
  48.1 52.5 %all-to-all-start = ((bf16[16,2,32768]{2,1,0:T(2,128)(2,1)}), bf16[16,2,32768]{2,1,0:T(2,128)(2,1)S(1)}, u32[]{:S(2)}, u32[]{:S(2)}) async-start(bf16[16,2,32768]{2,1,0:T(2,128)(2,1)} %reshape.118), calls=%async_computation | async-start | bytes 4194304 | tf_op jit(solution)/shard_map/all_to_all | solution.py:17
  114.2 2.0 copy-start
  114.2 2.2 copy-start.1
  118.2 1.2 copy-start.3
  119.4 1.8 copy-start.2
  127.3 1.2 copy-start.3
  128.6 1.8 copy-start.2
  136.5 1.2 copy-start.3
  137.8 1.7 copy-start.2
  145.6 1.2 copy-start.3
  146.9 1.7 copy-start.2
  192.7 11.8 %all-to-all-start.4 = ((f32[16,2,1024]{2,1,0:T(2,128)}), f32[16,2,1024]{2,1,0:T(2,128)S(1)}, u32[]{:S(2)}, u32[]{:S(2)}) async-start(f32[16,2,1024]{2,1,0:T(2,128)} %broadcast_in_dim.44), calls=%async_computation.4 | async-start | bytes 262144 | tf_op jit(solution)/shard_map/all_to_all | solution.py:23
  204.6 31.4 %all-to-all-start.2 = ((bf16[2,1024,256]{2,0,1:T(2,128)(2,1)}), bf16[2,1024,256]{2,0,1:T(2,128)(2,1)S(1)}, u32[]{:S(2)}, u32[]{:S(2)}) async-start(bf16[2,1024,256]{2,0,1:T(2,128)(2,1)} %copy.127), calls=%async_computation.2 | async-start | bytes 2097152 | tf_op jit(solution)/shard_map/all_to_all | solution.py:136
  236.8 24.4 %all-to-all-start.5 = ((f32[32,1,2304]{2,1,0:T(1,128)}), f32[32,1,2304]{2,1,0:T(1,128)S(1)}, u32[]{:S(2)}, u32[]{:S(2)}) async-start(f32[32,1,2304]{2,1,0:T(1,128)} %broadcast_in_dim.45), calls=%async_computation.5 | async-start | bytes 589824 | tf_op jit(solution)/shard_map/all_to_all | solution.py:23
where the time goes:
time: 264 us; the launch traced here: 263 us
  waiting for transfers between devices  95.4 us (36%)
  local copies, waits for them, and re-layouts  53.6 us (20%)
  blocking collectives  33.4 us (13%)
  starting transfers between devices  32.2 us (12%)
  matrix products  31.6 us (12%)
  other arithmetic  15.5 us (6%)
    all_to_all x2, waiting for transfers between devices, in_one_piece(): lax.all_to_all(both, axis, split_axis=split_dim, concat_axis=concat_dim,...  55.6 us
    all_to_all x1, blocking collectives, in_one_piece(): lax.all_to_all(both, axis, split_axis=split_dim, concat_axis=concat_dim,...  33.4 us
    all_to_all x1, waiting for transfers between devices, per_device(): lax.all_to_all(query_back, 'ctx', split_axis=1, concat_axis=2, tiled=True)  27.7 us
    unnamed x17, local copies, waits for them, and re-layouts  17.9 us
    all_to_all x2, starting transfers between devices, sent_to_all(): lax.all_to_all(jnp.broadcast_to(value[None], (length, *value.shape)), axi...  14.5 us
    all_to_all x2, starting transfers between devices, in_one_piece(): lax.all_to_all(both, axis, split_axis=split_dim, concat_axis=concat_dim,...  14.1 us
    all_to_all x2, waiting for transfers between devices, sent_to_all(): lax.all_to_all(jnp.broadcast_to(value[None], (length, *value.shape)), axi...  12 us
    all_to_all x2, local copies, waits for them, and re-layouts, in_one_piece(): lax.all_to_all(both, axis, split_axis=split_dim, concat_axis=concat_dim,...  8.32 us
  transfers between devices with their start and end apart: 5, of which 5 were waited for; matrix products, arithmetic and copies ran while one was open for 11% of the time, Pallas kernels for 0%

commit v1 on v0

v1 whole, which is shorter than its diff:
```python
import math

import jax
import jax.numpy as jnp
from jax import lax
from jax.experimental import pallas as pl
from jax.experimental.pallas import tpu as pltpu
from jax.sharding import PartitionSpec as P

HD = 128
NB = 16
GROUP = 4
CHIPS = 8
CORES = 2
CTX = CHIPS * CORES
DP = 32
TOK = 64
DOCS = 2
SLOTS = 8
TILE = 4
QW = GROUP * HD
INV_ROOT = 1.0 / math.sqrt(HD)
EXP_SCALE = INV_ROOT * math.log2(math.e)

F32 = jnp.float32
BF16 = jnp.bfloat16


def nt(a, b):
    return lax.dot_general(a, b, (((1,), (1,)), ((), ())), preferred_element_type=F32)


def nn(a, b):
    return lax.dot_general(a, b, (((1,), (0,)), ((), ())), preferred_element_type=F32)


def kernel(
    q_hbm, k_hbm, v_hbm, o_hbm, masked, bucket,
    dq_out, dk_out, dv_out, bias_out,
    q_in, k_in, v_in, o_in, qc_stage, kv_stage, qc_buf, kv_buf, dq_stage, dkv_stage, dkv_buf,
    kt, dk_acc, dv_acc, bias_src, bias_all, msg, dp_buf,
    in_sem, qc_send, qc_recv, kv_send, kv_recv, dq_send, dq_recv, dkv_send, dkv_recv, bias_sem, dp_sem,
):
    me = lax.axis_index("ctx")
    dp = lax.axis_index("dp")
    y, c = lax.div(me, 2), lax.rem(me, 2)

    loads = [
        pltpu.make_async_copy(src, dst, in_sem.at[n])
        for n, (src, dst) in enumerate(((k_hbm, k_in), (v_hbm, v_in), (q_hbm, q_in), (o_hbm, o_in)))
    ]
    for load in loads:
        load.start()

    barrier = pltpu.get_barrier_semaphore()

    def greet_ctx(s, _):
        pl.semaphore_signal(barrier, inc=1, device_id={"ctx": lax.rem(me + s, CTX)})
        return 0

    def greet_dp(s, _):
        pl.semaphore_signal(barrier, inc=1, device_id={"dp": lax.rem(dp + s, DP)})
        return 0

    lax.fori_loop(1, CTX, greet_ctx, 0)
    lax.fori_loop(1, DP, greet_dp, 0)

    def remote(src, dst, send, recv, device):
        return pltpu.make_async_remote_copy(
            src_ref=src, dst_ref=dst, send_sem=send, recv_sem=recv, device_id=device
        )

    def far_first(n):
        half = lax.div(n + 1, 2)
        return 8 + half * (2 * lax.rem(n, 2) - 1)

    loads[0].wait()
    loads[1].wait()
    for d in range(DOCS):
        for g in range(CHIPS):
            kv_stage[d, g, :, 0:HD] = k_in[d, :, g * HD : (g + 1) * HD]
            kv_stage[d, g, :, HD : 2 * HD] = v_in[d, :, g * HD : (g + 1) * HD]

    pl.semaphore_wait(barrier, CTX - 1 + DP - 1)

    def send_kv(k):
        own = lax.rem(y, 4) + 4 * k
        pltpu.make_async_copy(kv_stage.at[c, own], kv_buf.at[k, me], kv_recv.at[k]).start()

        def one(n, _):
            j = lax.rem(me + far_first(n), CTX)
            d = lax.rem(j, 2)
            g = lax.rem(lax.div(j, 2), 4) + 4 * k
            remote(
                kv_stage.at[d, g], kv_buf.at[k, me], kv_send.at[k], kv_recv.at[k], {"ctx": j}
            ).start()
            return 0

        lax.fori_loop(0, CTX - 1, one, 0)

    def send_qc(k):
        own = lax.rem(y, 4) + 4 * k
        for a, step in ((3, 2 + 4 * c), (1, 1), (2, 7)):
            t = lax.rem(y + step, CHIPS)
            g = lax.rem(t, 4) + 4 * k
            for d in range(DOCS):
                remote(
                    qc_stage.at[d, g], qc_buf.at[k, 2 * a + c], qc_send.at[k], qc_recv.at[k],
                    {"ctx": 2 * t + d},
                ).start()
        remote(
            qc_stage.at[1 - c, own], qc_buf.at[k, c], qc_send.at[k], qc_recv.at[k],
            {"ctx": 2 * y + 1 - c},
        ).start()
        pltpu.make_async_copy(qc_stage.at[c, own], qc_buf.at[k, c], qc_recv.at[k]).start()

    send_kv(0)

    loads[2].wait()
    loads[3].wait()
    rows = lax.broadcasted_iota(jnp.int32, (TOK, 1), 0)
    diagonal = lax.broadcasted_iota(jnp.int32, (TOK, TOK), 0) == lax.broadcasted_iota(
        jnp.int32, (TOK, TOK), 1
    )
    for d in range(DOCS):
        hit = masked[d : d + 1, :] == rows + me * TOK
        is_masked = jnp.max(jnp.where(hit, 1.0, 0.0), axis=1, keepdims=True)
        row = bucket[d : d + 1, :].astype(F32)
        column = jnp.sum(jnp.where(diagonal, row, 0.0), axis=1, keepdims=True)
        weight = is_masked * NB / (column + 1.0)
        for g in range(CHIPS):
            qc_stage[d, g, :, 0:QW] = q_in[d, :, g * QW : (g + 1) * QW]
            grads = o_in[d, :, g * QW : (g + 1) * QW].astype(F32)
            qc_stage[d, g, :, QW : 2 * QW] = (grads * weight).astype(BF16)

    send_qc(0)
    send_kv(1)
    send_qc(1)

    def whole(ref, sem):
        pltpu.make_async_copy(ref, ref, sem).wait()

    bias_src[...] = jnp.zeros_like(bias_src)
    for k in range(2):
        own = lax.rem(y, 4) + 4 * k
        whole(kv_buf.at[k], kv_recv.at[k])
        whole(qc_buf.at[k], qc_recv.at[k])
        kt[...] = kv_buf[k, :, :, 0:HD].reshape(CTX * TOK, HD).T
        dk_acc[...] = jnp.zeros_like(dk_acc)
        dv_acc[...] = jnp.zeros_like(dv_acc)

        def step(n, _):
            h, part = lax.div(n, 2), lax.rem(n, 2)
            slots = pl.ds(part * TILE, TILE)
            q_cols = pl.ds(pl.multiple_of(h * HD, HD), HD)
            c_cols = pl.ds(pl.multiple_of(h * HD + QW, HD), HD)
            q = qc_buf[k, slots, :, q_cols].reshape(TILE * TOK, HD)
            cot = qc_buf[k, slots, :, c_cols].reshape(TILE * TOK, HD)
            keys = kv_buf[k, :, :, 0:HD].reshape(CTX * TOK, HD)
            values = kv_buf[k, :, :, HD : 2 * HD].reshape(CTX * TOK, HD)
            scores = nt(keys, q)
            top = jnp.max(scores, axis=0, keepdims=True)
            exponent = jnp.exp2((scores - top) * EXP_SCALE)
            probs = exponent * (1.0 / jnp.sum(exponent, axis=0, keepdims=True))
            probs_low = probs.astype(BF16)
            prob_grad = nt(values, cot)
            delta = jnp.sum(probs_low.astype(F32) * prob_grad, axis=0, keepdims=True)
            score_grad = (probs * (prob_grad - delta) * INV_ROOT).astype(BF16)
            dv_acc[...] += nn(probs_low, cot)
            dk_acc[...] += nn(score_grad, q)
            grad = nn(kt[...], score_grad).T
            dq_stage[k, slots, :, q_cols] = grad.astype(BF16).reshape(TILE, TOK, HD)
            bias_src[pl.ds(k * GROUP + h, 1), :] += jnp.sum(grad, axis=0, keepdims=True)
            return 0

        lax.fori_loop(0, GROUP * SLOTS // TILE, step, 0)
        bias_src[8 + k : 9 + k, :] = jnp.sum(dk_acc[...], axis=0, keepdims=True)
        bias_src[10 + k : 11 + k, :] = jnp.sum(dv_acc[...], axis=0, keepdims=True)
        dkv_stage[k, :, :, 0:HD] = dk_acc[...].astype(BF16).reshape(CTX, TOK, HD)
        dkv_stage[k, :, :, HD : 2 * HD] = dv_acc[...].astype(BF16).reshape(CTX, TOK, HD)

        if k == 1:
            pltpu.make_async_copy(bias_src, bias_all.at[me], bias_sem.at[1]).start()

            def send_bias(s, _):
                remote(
                    bias_src, bias_all.at[me], bias_sem.at[0], bias_sem.at[1],
                    {"ctx": lax.rem(me + s, CTX)},
                ).start()
                return 0

            lax.fori_loop(1, CTX, send_bias, 0)

        centre = lax.div(y, 4)

        def send_dkv(n, _):
            j = lax.rem(me + far_first(n), CTX)
            remote(
                dkv_stage.at[k, j], dkv_buf.at[centre, c, own], dkv_send.at[k], dkv_recv,
                {"ctx": j},
            ).start()
            return 0

        lax.fori_loop(0, CTX - 1, send_dkv, 0)
        pltpu.make_async_copy(
            dkv_stage.at[k, me], dkv_buf.at[centre, c, own], dkv_recv
        ).start()

        out_cols = pl.ds(pl.multiple_of(own * QW, QW), QW)
        for a, back in ((3, None), (1, 7), (2, 1)):
            for core in range(CORES):
                step_back = 6 - 4 * core if back is None else back
                j = 2 * lax.rem(y + step_back, CHIPS) + core
                remote(
                    dq_stage.at[k, 2 * a + core], dq_out.at[c, :, out_cols], dq_send.at[k],
                    dq_recv, {"ctx": j},
                ).start()
        remote(
            dq_stage.at[k, 1 - c], dq_out.at[c, :, out_cols], dq_send.at[k], dq_recv,
            {"ctx": 2 * y + 1 - c},
        ).start()
        pltpu.make_async_copy(dq_stage.at[k, c], dq_out.at[c, :, out_cols], dq_recv).start()

    whole(bias_all, bias_sem.at[1])
    first = lax.rem(y, 4) * 2
    q_row = lax.div(y, 4) * GROUP + 2 * c
    msg[...] = jnp.zeros_like(msg)
    for b in range(2):
        total = sum(bias_all[first + n, pl.ds(q_row + b, 1), :] for n in (0, 1, 8, 9))
        for a in range(4 * b, 4 * b + 4):
            msg[a, 0:1, :] = total
    for g in range(CHIPS):
        m, k = g % 4, g // 4
        for row, at in ((1, 8 + k), (2, 10 + k)):
            msg[g, row : row + 1, :] = sum(
                bias_all[2 * m + n, at : at + 1, :] for n in (0, 1, 8, 9)
            )
    pltpu.make_async_copy(msg.at[lax.div(dp, 4)], dp_buf.at[dp], dp_sem.at[1]).start()

    def send_msg(s, _):
        j = lax.rem(dp + s, DP)
        remote(
            msg.at[lax.div(j, 4)], dp_buf.at[dp], dp_sem.at[0], dp_sem.at[1], {"dp": j}
        ).start()
        return 0

    lax.fori_loop(1, DP, send_msg, 0)

    whole(dkv_buf, dkv_recv)
    for d in range(DOCS):
        for g in range(CHIPS):
            both = dkv_buf[0, d, g].astype(F32) + dkv_buf[1, d, g].astype(F32)
            dk_out[d, :, g * HD : (g + 1) * HD] = both[:, 0:HD].astype(BF16)
            dv_out[d, :, g * HD : (g + 1) * HD] = both[:, HD : 2 * HD].astype(BF16)

    whole(dp_buf, dp_sem.at[1])
    bias_out[...] = jnp.sum(dp_buf[...], axis=0) * (1.0 / 256.0)
    whole(dq_out, dq_recv)

    for k in range(2):
        whole(kv_buf.at[k, pl.ds(0, CTX - 1)], kv_send.at[k])
        whole(qc_buf.at[k, pl.ds(0, SLOTS - 1)], qc_send.at[k])
        whole(dkv_stage.at[k, pl.ds(0, CTX - 1)], dkv_send.at[k])
        whole(dq_stage.at[k, pl.ds(0, SLOTS - 1)], dq_send.at[k])
    whole(bias_all.at[pl.ds(0, CTX - 1)], bias_sem.at[0])
    whole(dp_buf.at[pl.ds(0, DP - 1)], dp_sem.at[0])


def per_device(query, key_in, value_in, out_grad, masked, bucket):
    vmem = pl.BlockSpec(memory_space=pltpu.VMEM)
    hbm = pl.BlockSpec(memory_space=pl.ANY)
    dma = pltpu.SemaphoreType.DMA
    query_grad, key_grad, value_grad, bias = pl.pallas_call(
        kernel,
        out_shape=(
            jax.ShapeDtypeStruct(query.shape, BF16),
            jax.ShapeDtypeStruct(key_in.shape, BF16),
            jax.ShapeDtypeStruct(value_in.shape, BF16),
            jax.ShapeDtypeStruct((8, HD), F32),
        ),
        in_specs=[hbm, hbm, hbm, hbm, vmem, vmem],
        out_specs=(hbm, vmem, vmem, vmem),
        scratch_shapes=[
            pltpu.VMEM(query.shape, BF16),
            pltpu.VMEM(key_in.shape, BF16),
            pltpu.VMEM(value_in.shape, BF16),
            pltpu.VMEM(out_grad.shape, BF16),
            pltpu.VMEM((DOCS, CHIPS, TOK, 2 * QW), BF16),
            pltpu.VMEM((DOCS, CHIPS, TOK, 2 * HD), BF16),
            pltpu.VMEM((2, SLOTS, TOK, 2 * QW), BF16),
            pltpu.VMEM((2, CTX, TOK, 2 * HD), BF16),
            pltpu.VMEM((2, SLOTS, TOK, QW), BF16),
            pltpu.VMEM((2, CTX, TOK, 2 * HD), BF16),
            pltpu.VMEM((2, DOCS, CHIPS, TOK, 2 * HD), BF16),
            pltpu.VMEM((HD, CTX * TOK), BF16),
            pltpu.VMEM((CTX * TOK, HD), F32),
            pltpu.VMEM((CTX * TOK, HD), F32),
            pltpu.VMEM((16, HD), F32),
            pltpu.VMEM((CTX, 16, HD), F32),
            pltpu.VMEM((CHIPS, 8, HD), F32),
            pltpu.VMEM((DP, 8, HD), F32),
            dma((4,)),
            dma((2,)),
            dma((2,)),
            dma((2,)),
            dma((2,)),
            dma((2,)),
            dma,
            dma((2,)),
            dma,
            dma((2,)),
            dma((2,)),
        ],
        compiler_params=pltpu.CompilerParams(
            collective_id=0, has_side_effects=True, vmem_limit_bytes=40 * 1024 * 1024
        ),
        cost_estimate=pl.CostEstimate(
            flops=6 * 10**9, bytes_accessed=8 * 10**6, transcendentals=4 * 10**6
        ),
    )(query, key_in, value_in, out_grad, masked, bucket)
    dp = lax.axis_index("dp")
    query_piece = lax.dynamic_slice(bias, (0, 8 * (dp % 16)), (1, 8))
    pair_piece = lax.dynamic_slice(bias, (1, 32 * (dp % 4)), (2, 32))
    return query_grad, key_grad, value_grad, query_piece, pair_piece


def solution(mesh):
    tokens = P("dp", "ctx", None)
    return jax.shard_map(
        per_device,
        mesh=mesh,
        in_specs=(tokens, tokens, tokens, tokens, P("dp", None), P("dp", "ctx")),
        out_specs=(tokens, tokens, tokens, P("ctx", "dp"), P(None, "dp")),
        check_vma=False,
    )
```

time: 264 us -> 109 us (0.41)
  Pallas kernels: 0 us -> 99.5 us
  waiting for transfers between devices: 95.4 us -> 0 us
  local copies, waits for them, and re-layouts: 53.6 us -> 8.61 us
  blocking collectives: 33.4 us -> 0 us
  starting transfers between devices: 32.2 us -> 0 us
  matrix products: 31.6 us -> 0 us
  other arithmetic: 15.5 us -> 0 us
    pallas_call x0 -> x1, Pallas kernels: none -> 99.5 us  [per_device(): pl.pallas_call(kernel, out_shape=(jax.ShapeDtypeStruct(query.shape, BF16)...]
    all_to_all x5 -> x0, waiting for transfers between devices: 95.4 us -> none  [the longest x2 55.6 us: in_one_piece(): lax.all_to_all(both, axis, split_axis=split_dim, concat_axis=concat_dim,...]
    all_to_all x1 -> x0, blocking collectives: 33.4 us -> none  [in_one_piece(): lax.all_to_all(both, axis, split_axis=split_dim, concat_axis=concat_dim,...]
    all_to_all x5 -> x0, starting transfers between devices: 32.2 us -> none  [the longest x2 14.5 us: sent_to_all(): lax.all_to_all(jnp.broadcast_to(value[None], (length, *value.shape)), axi...]
    dot_general x24 -> x0, matrix products: 31.6 us -> none  [the longest x4 6.99 us: head_pass(): jnp.einsum('qk,qd->kd', probs_low, cot_one, preferred_element_type=jnp.fl...]
    reduce_sum x13 -> x0, other arithmetic: 10.7 us -> none  [the longest x4 2.93 us: softmax_rows(): return exponent / jnp.sum(exponent, axis=-1, keepdims=True)]
    unnamed x17 -> x15, local copies, waits for them, and re-layouts: 17.9 us -> 7.4 us
    all_to_all x4 -> x0, local copies, waits for them, and re-layouts: 9.53 us -> none  [the longest x2 8.32 us: in_one_piece(): lax.all_to_all(both, axis, split_axis=split_dim, concat_axis=concat_dim,...]
  transfers between devices with their start and end apart: 5 -> 0, of which waited for: 5 -> 0; matrix products, arithmetic and copies ran while one was open for 11% -> 0% of each run, Pallas kernels for 0% -> 0%
where the time goes in v1:
time: 109 us
  Pallas kernels  99.5 us (91%)
  local copies, waits for them, and re-layouts  8.61 us (8%)
    pallas_call x1, Pallas kernels, per_device(): pl.pallas_call(kernel, out_shape=(jax.ShapeDtypeStruct(query.shape, BF16)...  99.5 us
    unnamed x15, local copies, waits for them, and re-layouts  7.4 us

profile of v1, /device:TPU:1, one launch (start us, length us, event | category | flops | bytes accessed | tf_op | source)
XLA Modules:
  0.0 108.8 jit_solution(9793414139873441055)
XLA Ops:
  0.6 0.0 copy-start.4
  0.7 0.0 copy-start.5
  0.7 0.7 copy-done.4
  1.3 0.0 copy-done.5
  1.3 0.0 copy-start
  1.3 1.2 %copy-done = bf16[2,64,4096]{2,1,0:T(8,128)(2,1)S(1)} copy-done((bf16[2,64,4096]{2,1,0:T(8,128)(2,1)S(1)}, bf16[2,64,4096]{2,1,0:T(8,128)(2,1)}, u32[]{:S(2)}) %copy-start) | copy-done | bytes 1048600
  2.6 0.0 copy-start.1
  2.6 1.2 %copy-done.1 = bf16[2,64,4096]{2,1,0:T(8,128)(2,1)S(1)} copy-done((bf16[2,64,4096]{2,1,0:T(8,128)(2,1)S(1)}, bf16[2,64,4096]{2,1,0:T(8,128)(2,1)}, u32[]{:S(2)}) %copy-start.1) | copy-done | bytes 1048600
  3.8 0.0 copy-start.2
  3.8 0.9 copy-done.2
  4.7 0.0 copy-start.3
  4.7 0.9 copy-done.3
  5.7 99.5 %shard_map.101 = (bf16[2,64,4096]{2,1,0:T(8,128)(2,1)S(1)}, bf16[2,64,1024]{2,1,0:T(8,128)(2,1)S(1)}, bf16[2,64,1024]{2,1,0:T(8,128)(2,1)S(1)}, f32[8,128]{1,0:T(8,128)S(1)}) custom-call(bf16[2,64,4096]{2,1,0:T(8,128)(2,1)S(1)} %copy-done, bf16[2,64,1024]{2,1,0:T(8,128)(2,1)S(1)} %copy-done.2, bf16[2,64,1024]{2,1,0:T(8,128)(2,1)S(1)} %copy-done.3, ...), custom_call_target="tpu_custom_call" | custom-call | flops 6000000000 | bytes 8000000 | tf_op jit(solution)/shard_map/pallas_call | solution.py:273
  105.2 0.6 constant_dynamic-slice_fusion
  105.8 0.6 constant_dynamic-slice_fusion.1
  106.4 1.0 copy.14
  107.4 0.7 copy.15
  108.1 0.7 copy.16
Async XLA Ops:
  0.6 0.7 copy-start.4
  0.7 0.7 copy-start.5
  1.3 1.2 %copy-start = (bf16[2,64,4096]{2,1,0:T(8,128)(2,1)S(1)}, bf16[2,64,4096]{2,1,0:T(8,128)(2,1)}, u32[]{:S(2)}) copy-start(bf16[2,64,4096]{2,1,0:T(8,128)(2,1)} %q_hbm.1) | copy-start | bytes 3145732
  2.6 1.2 %copy-start.1 = (bf16[2,64,4096]{2,1,0:T(8,128)(2,1)S(1)}, bf16[2,64,4096]{2,1,0:T(8,128)(2,1)}, u32[]{:S(2)}) copy-start(bf16[2,64,4096]{2,1,0:T(8,128)(2,1)} %o_hbm.1) | copy-start | bytes 3145732
  3.8 0.9 copy-start.2
  4.7 0.9 copy-start.3

commit v2 on v1

--- a/solution.py
+++ b/solution.py
@@ -18,6 +18,7 @@
 DOCS = 2
 SLOTS = 8
 TILE = 4
+AHEAD = 5
 QW = GROUP * HD
 INV_ROOT = 1.0 / math.sqrt(HD)
 EXP_SCALE = INV_ROOT * math.log2(math.e)
@@ -35,11 +36,12 @@
 
 
 def kernel(
-    q_hbm, k_hbm, v_hbm, o_hbm, masked, bucket,
-    dq_out, dk_out, dv_out, bias_out,
-    q_in, k_in, v_in, o_in, qc_stage, kv_stage, qc_buf, kv_buf, dq_stage, dkv_stage, dkv_buf,
-    kt, dk_acc, dv_acc, bias_src, bias_all, msg, dp_buf,
-    in_sem, qc_send, qc_recv, kv_send, kv_recv, dq_send, dq_recv, dkv_send, dkv_recv, bias_sem, dp_sem,
+    q_hbm, k_hbm, v_hbm, o_hbm, masked_hbm, bucket_hbm,
+    dq_out, dkv_out, bias_out,
+    q_in, k_in, v_in, o_in, masked, bucket, qc_stage, kv_stage, qc_buf, kv_buf, dq_stage, dkv_stage,
+    kt, dk_acc, dv_acc, bias_src, bias_all, msg, dp_buf, bias_sum, bias_in,
+    in_sem, qc_send, qc_recv, kv_send, kv_recv, dq_send, dq_recv, dkv_send, dkv_recv,
+    bias_send, bias_recv, dp_sem, share_sem, go_sem,
 ):
     me = lax.axis_index("ctx")
     dp = lax.axis_index("dp")
@@ -47,23 +49,32 @@
 
     loads = [
         pltpu.make_async_copy(src, dst, in_sem.at[n])
-        for n, (src, dst) in enumerate(((k_hbm, k_in), (v_hbm, v_in), (q_hbm, q_in), (o_hbm, o_in)))
+        for n, (src, dst) in enumerate(
+            (
+                (k_hbm, k_in), (v_hbm, v_in), (q_hbm, q_in), (o_hbm, o_in),
+                (masked_hbm, masked), (bucket_hbm, bucket),
+            )
+        )
     ]
     for load in loads:
         load.start()
 
     barrier = pltpu.get_barrier_semaphore()
 
-    def greet_ctx(s, _):
-        pl.semaphore_signal(barrier, inc=1, device_id={"ctx": lax.rem(me + s, CTX)})
+    def greet_other(n, _):
+        pl.semaphore_signal(barrier, inc=1, device_id={"ctx": 2 * lax.rem(y + n, CHIPS)})
         return 0
 
     def greet_dp(s, _):
         pl.semaphore_signal(barrier, inc=1, device_id={"dp": lax.rem(dp + s, DP)})
         return 0
 
-    lax.fori_loop(1, CTX, greet_ctx, 0)
-    lax.fori_loop(1, DP, greet_dp, 0)
+    lax.fori_loop(1, CHIPS, greet_other, 0)
+
+    @pl.when(c == 1)
+    def _():
+        pl.semaphore_signal(barrier, inc=1, device_id={"ctx": me - 1})
+        lax.fori_loop(1, DP, greet_dp, 0)
 
     def remote(src, dst, send, recv, device):
         return pltpu.make_async_remote_copy(
@@ -81,7 +92,14 @@
             kv_stage[d, g, :, 0:HD] = k_in[d, :, g * HD : (g + 1) * HD]
             kv_stage[d, g, :, HD : 2 * HD] = v_in[d, :, g * HD : (g + 1) * HD]
 
-    pl.semaphore_wait(barrier, CTX - 1 + DP - 1)
+    @pl.when(c == 0)
+    def _():
+        pl.semaphore_wait(barrier, CTX - 1)
+        pl.semaphore_signal(go_sem, inc=1, device_id={"ctx": me + 1})
+
+    @pl.when(c == 1)
+    def _():
+        pl.semaphore_wait(go_sem, 1)
 
     def send_kv(k):
         own = lax.rem(y, 4) + 4 * k
@@ -116,8 +134,8 @@
 
     send_kv(0)
 
-    loads[2].wait()
-    loads[3].wait()
+    for load in loads[2:]:
+        load.wait()
     rows = lax.broadcasted_iota(jnp.int32, (TOK, 1), 0)
     diagonal = lax.broadcasted_iota(jnp.int32, (TOK, TOK), 0) == lax.broadcasted_iota(
         jnp.int32, (TOK, TOK), 1
@@ -139,6 +157,36 @@
 
     def whole(ref, sem):
         pltpu.make_async_copy(ref, ref, sem).wait()
+
+    def reduce_bias():
+        for k in range(2):
+            whole(bias_all.at[k], bias_recv.at[k])
+        first = lax.rem(y, 4) * 2
+        msg[...] = jnp.zeros_like(msg)
+        for core in range(CORES):
+            for b in range(2):
+                row = 2 * core + b
+                total = sum(
+                    bias_all[lax.div(y, 4), first + n, row : row + 1, :] for n in (0, 1, 8, 9)
+                )
+                for a in range(4 * b, 4 * b + 4):
+                    msg[a, core : core + 1, :] = total
+        for g in range(CHIPS):
+            m, k = g % 4, g // 4
+            msg[g, 2:4, :] = sum(
+                bias_all[k, 2 * m + n, GROUP : GROUP + 2, :] for n in (0, 1, 8, 9)
+            )
+        pl.semaphore_wait(barrier, DP - 1)
+        pltpu.make_async_copy(msg.at[lax.div(dp, 4)], dp_buf.at[dp], dp_sem.at[1]).start()
+
+        def send_msg(s, _):
+            j = lax.rem(dp + s, DP)
+            remote(
+                msg.at[lax.div(j, 4)], dp_buf.at[dp], dp_sem.at[0], dp_sem.at[1], {"dp": j}
+            ).start()
+            return 0
+
+        lax.fori_loop(1, DP, send_msg, 0)
 
     bias_src[...] = jnp.zeros_like(bias_src)
     for k in range(2):
@@ -170,41 +218,34 @@
             dk_acc[...] += nn(score_grad, q)
             grad = nn(kt[...], score_grad).T
             dq_stage[k, slots, :, q_cols] = grad.astype(BF16).reshape(TILE, TOK, HD)
-            bias_src[pl.ds(k * GROUP + h, 1), :] += jnp.sum(grad, axis=0, keepdims=True)
+            bias_src[k, pl.ds(h, 1), :] += jnp.sum(grad, axis=0, keepdims=True)
             return 0
 
         lax.fori_loop(0, GROUP * SLOTS // TILE, step, 0)
-        bias_src[8 + k : 9 + k, :] = jnp.sum(dk_acc[...], axis=0, keepdims=True)
-        bias_src[10 + k : 11 + k, :] = jnp.sum(dv_acc[...], axis=0, keepdims=True)
+        bias_src[k, GROUP : GROUP + 1, :] = jnp.sum(dk_acc[...], axis=0, keepdims=True)
+        bias_src[k, GROUP + 1 : GROUP + 2, :] = jnp.sum(dv_acc[...], axis=0, keepdims=True)
         dkv_stage[k, :, :, 0:HD] = dk_acc[...].astype(BF16).reshape(CTX, TOK, HD)
         dkv_stage[k, :, :, HD : 2 * HD] = dv_acc[...].astype(BF16).reshape(CTX, TOK, HD)
 
-        if k == 1:
-            pltpu.make_async_copy(bias_src, bias_all.at[me], bias_sem.at[1]).start()
-
-            def send_bias(s, _):
-                remote(
-                    bias_src, bias_all.at[me], bias_sem.at[0], bias_sem.at[1],
-                    {"ctx": lax.rem(me + s, CTX)},
-                ).start()
-                return 0
-
-            lax.fori_loop(1, CTX, send_bias, 0)
-
-        centre = lax.div(y, 4)
-
-        def send_dkv(n, _):
-            j = lax.rem(me + far_first(n), CTX)
+        def send_bias(n, _):
             remote(
-                dkv_stage.at[k, j], dkv_buf.at[centre, c, own], dkv_send.at[k], dkv_recv,
-                {"ctx": j},
+                bias_src.at[k], bias_all.at[k, me], bias_send.at[k], bias_recv.at[k],
+                {"ctx": 2 * lax.rem(y + n, CHIPS) + 1},
             ).start()
             return 0
 
-        lax.fori_loop(0, CTX - 1, send_dkv, 0)
-        pltpu.make_async_copy(
-            dkv_stage.at[k, me], dkv_buf.at[centre, c, own], dkv_recv
-        ).start()
+        lax.fori_loop(1, CHIPS, send_bias, 0)
+
+        @pl.when(c == 0)
+        def _():
+            remote(
+                bias_src.at[k], bias_all.at[k, me], bias_send.at[k], bias_recv.at[k],
+                {"ctx": me + 1},
+            ).start()
+
+        @pl.when(c == 1)
+        def _():
+            pltpu.make_async_copy(bias_src.at[k], bias_all.at[k, me], bias_recv.at[k]).start()
 
         out_cols = pl.ds(pl.multiple_of(own * QW, QW), QW)
         for a, back in ((3, None), (1, 7), (2, 1)):
@@ -221,85 +262,116 @@
         ).start()
         pltpu.make_async_copy(dq_stage.at[k, c], dq_out.at[c, :, out_cols], dq_recv).start()
 
-    whole(bias_all, bias_sem.at[1])
-    first = lax.rem(y, 4) * 2
-    q_row = lax.div(y, 4) * GROUP + 2 * c
-    msg[...] = jnp.zeros_like(msg)
-    for b in range(2):
-        total = sum(bias_all[first + n, pl.ds(q_row + b, 1), :] for n in (0, 1, 8, 9))
-        for a in range(4 * b, 4 * b + 4):
-            msg[a, 0:1, :] = total
-    for g in range(CHIPS):
-        m, k = g % 4, g // 4
-        for row, at in ((1, 8 + k), (2, 10 + k)):
-            msg[g, row : row + 1, :] = sum(
-                bias_all[2 * m + n, at : at + 1, :] for n in (0, 1, 8, 9)
-            )
-    pltpu.make_async_copy(msg.at[lax.div(dp, 4)], dp_buf.at[dp], dp_sem.at[1]).start()
-
-    def send_msg(s, _):
-        j = lax.rem(dp + s, DP)
-        remote(
-            msg.at[lax.div(j, 4)], dp_buf.at[dp], dp_sem.at[0], dp_sem.at[1], {"dp": j}
+        centre = lax.div(y, 4)
+
+        def send_dkv(n, _):
+            j = lax.rem(me + far_first(n), CTX)
+            remote(
+                dkv_stage.at[k, j], dkv_out.at[centre, c, own], dkv_send.at[k], dkv_recv,
+                {"ctx": j},
+            ).start()
+            return 0
+
+        ahead = 15 if k == 0 else AHEAD
+        lax.fori_loop(0, ahead, send_dkv, 0)
+        if k == 1:
+            pl.when(c == 1)(reduce_bias)
+        lax.fori_loop(ahead, CTX - 1, send_dkv, 0)
+        pltpu.make_async_copy(
+            dkv_stage.at[k, me], dkv_out.at[centre, c, own], dkv_recv
         ).start()
-        return 0
-
-    lax.fori_loop(1, DP, send_msg, 0)
-
-    whole(dkv_buf, dkv_recv)
-    for d in range(DOCS):
-        for g in range(CHIPS):
-            both = dkv_buf[0, d, g].astype(F32) + dkv_buf[1, d, g].astype(F32)
-            dk_out[d, :, g * HD : (g + 1) * HD] = both[:, 0:HD].astype(BF16)
-            dv_out[d, :, g * HD : (g + 1) * HD] = both[:, HD : 2 * HD].astype(BF16)
-
-    whole(dp_buf, dp_sem.at[1])
-    bias_out[...] = jnp.sum(dp_buf[...], axis=0) * (1.0 / 256.0)
+
+    whole(dkv_out, dkv_recv)
     whole(dq_out, dq_recv)
+    @pl.when(c == 1)
+    def _():
+        whole(dp_buf, dp_sem.at[1])
+        bias_sum[...] = jnp.sum(dp_buf[...], axis=0) * (1.0 / 256.0)
+        share = remote(bias_sum, bias_in, share_sem.at[0], share_sem.at[1], {"ctx": me - 1})
+        share.start()
+        bias_out[...] = bias_sum[...]
+        share.wait_send()
+        whole(dp_buf.at[pl.ds(0, DP - 1)], dp_sem.at[0])
+
+    @pl.when(c == 0)
+    def _():
+        whole(bias_in, share_sem.at[1])
+        bias_out[...] = bias_in[...]
+
 
     for k in range(2):
         whole(kv_buf.at[k, pl.ds(0, CTX - 1)], kv_send.at[k])
         whole(qc_buf.at[k, pl.ds(0, SLOTS - 1)], qc_send.at[k])
         whole(dkv_stage.at[k, pl.ds(0, CTX - 1)], dkv_send.at[k])
         whole(dq_stage.at[k, pl.ds(0, SLOTS - 1)], dq_send.at[k])
-    whole(bias_all.at[pl.ds(0, CTX - 1)], bias_sem.at[0])
-    whole(dp_buf.at[pl.ds(0, DP - 1)], dp_sem.at[0])
+
+    @pl.when(c == 0)
+    def _():
+        for k in range(2):
+            whole(bias_all.at[k, pl.ds(0, CHIPS)], bias_send.at[k])
+
+    @pl.when(c == 1)
+    def _():
+        for k in range(2):
+            whole(bias_all.at[k, pl.ds(0, CHIPS - 1)], bias_send.at[k])
+
+
+def finish(dq, dkv, bias, dq_out, dk_out, dv_out, q_out, kv_out, sem):
+    copy = pltpu.make_async_copy(dq, dq_out, sem)
+    copy.start()
+    dp = lax.axis_index("dp")
+    first = lax.rem(lax.axis_index("ctx"), 2) == 0
+    q_rows = jnp.where(first, bias[0:1, :], bias[1:2, :])
+    q_out[...] = pltpu.roll(q_rows, lax.rem(HD - 8 * lax.rem(dp, 16), HD), 1)[:, 0:8]
+    kv_out[...] = pltpu.roll(bias[2:4, :], lax.rem(HD - 32 * lax.rem(dp, 4), HD), 1)[:, 0:32]
+    for d in range(DOCS):
+        for g in range(CHIPS):
+            both = dkv[0, d, g].astype(F32) + dkv[1, d, g].astype(F32)
+            dk_out[d, :, g * HD : (g + 1) * HD] = both[:, 0:HD].astype(BF16)
+            dv_out[d, :, g * HD : (g + 1) * HD] = both[:, HD : 2 * HD].astype(BF16)
+    copy.wait()
 
 
 def per_device(query, key_in, value_in, out_grad, masked, bucket):
     vmem = pl.BlockSpec(memory_space=pltpu.VMEM)
     hbm = pl.BlockSpec(memory_space=pl.ANY)
     dma = pltpu.SemaphoreType.DMA
-    query_grad, key_grad, value_grad, bias = pl.pallas_call(
+    args = (
+        pltpu.with_memory_space_constraint(x, pltpu.HBM)
+        for x in (query, key_in, value_in, out_grad, masked, bucket)
+    )
+    dq, dkv, bias = pl.pallas_call(
         kernel,
         out_shape=(
             jax.ShapeDtypeStruct(query.shape, BF16),
-            jax.ShapeDtypeStruct(key_in.shape, BF16),
-            jax.ShapeDtypeStruct(value_in.shape, BF16),
+            jax.ShapeDtypeStruct((2, DOCS, CHIPS, TOK, 2 * HD), BF16),
             jax.ShapeDtypeStruct((8, HD), F32),
         ),
-        in_specs=[hbm, hbm, hbm, hbm, vmem, vmem],
-        out_specs=(hbm, vmem, vmem, vmem),
+        in_specs=[hbm] * 6,
+        out_specs=(hbm, hbm, vmem),
         scratch_shapes=[
             pltpu.VMEM(query.shape, BF16),
             pltpu.VMEM(key_in.shape, BF16),
             pltpu.VMEM(value_in.shape, BF16),
             pltpu.VMEM(out_grad.shape, BF16),
+            pltpu.VMEM(masked.shape, jnp.int32),
+            pltpu.VMEM(bucket.shape, jnp.int32),
             pltpu.VMEM((DOCS, CHIPS, TOK, 2 * QW), BF16),
             pltpu.VMEM((DOCS, CHIPS, TOK, 2 * HD), BF16),
             pltpu.VMEM((2, SLOTS, TOK, 2 * QW), BF16),
             pltpu.VMEM((2, CTX, TOK, 2 * HD), BF16),
             pltpu.VMEM((2, SLOTS, TOK, QW), BF16),
             pltpu.VMEM((2, CTX, TOK, 2 * HD), BF16),
-            pltpu.VMEM((2, DOCS, CHIPS, TOK, 2 * HD), BF16),
             pltpu.VMEM((HD, CTX * TOK), BF16),
             pltpu.VMEM((CTX * TOK, HD), F32),
             pltpu.VMEM((CTX * TOK, HD), F32),
-            pltpu.VMEM((16, HD), F32),
-            pltpu.VMEM((CTX, 16, HD), F32),
+            pltpu.VMEM((2, 8, HD), F32),
+            pltpu.VMEM((2, CTX, 8, HD), F32),
             pltpu.VMEM((CHIPS, 8, HD), F32),
             pltpu.VMEM((DP, 8, HD), F32),
-            dma((4,)),
+            pltpu.VMEM((8, HD), F32),
+            pltpu.VMEM((8, HD), F32),
+            dma((6,)),
             dma((2,)),
             dma((2,)),
             dma((2,)),
@@ -310,6 +382,9 @@
             dma,
             dma((2,)),
             dma((2,)),
+            dma((2,)),
+            dma((2,)),
+            pltpu.SemaphoreType.REGULAR,
         ],
         compiler_params=pltpu.CompilerParams(
             collective_id=0, has_side_effects=True, vmem_limit_bytes=40 * 1024 * 1024
@@ -317,11 +392,21 @@
         cost_estimate=pl.CostEstimate(
             flops=6 * 10**9, bytes_accessed=8 * 10**6, transcendentals=4 * 10**6
         ),
-    )(query, key_in, value_in, out_grad, masked, bucket)
-    dp = lax.axis_index("dp")
-    query_piece = lax.dynamic_slice(bias, (0, 8 * (dp % 16)), (1, 8))
-    pair_piece = lax.dynamic_slice(bias, (1, 32 * (dp % 4)), (2, 32))
-    return query_grad, key_grad, value_grad, query_piece, pair_piece
+    )(*args)
+    return pl.pallas_call(
+        finish,
+        out_shape=(
+            jax.ShapeDtypeStruct(query.shape, BF16),
+            jax.ShapeDtypeStruct(key_in.shape, BF16),
+            jax.ShapeDtypeStruct(value_in.shape, BF16),
+            jax.ShapeDtypeStruct((1, 8), F32),
+            jax.ShapeDtypeStruct((2, 32), F32),
+        ),
+        in_specs=[hbm, vmem, vmem],
+        out_specs=(hbm, vmem, vmem, vmem, vmem),
+        scratch_shapes=[dma],
+        compiler_params=pltpu.CompilerParams(vmem_limit_bytes=32 * 1024 * 1024),
+    )(dq, dkv, bias)
 
 
 def solution(mesh):

time: 109 us -> 96.7 us (0.89)
  local copies, waits for them, and re-layouts: 8.61 us -> 0 us
  Pallas kernels: 99.5 us -> 95.9 us
    unnamed x15 -> x0, local copies, waits for them, and re-layouts: 7.4 us -> none
    pallas_call x1, Pallas kernels: 99.5 us -> 94.1 us  [per_device(): pl.pallas_call(kernel, out_shape=(jax.ShapeDtypeStruct(query.shape, BF16)...]
    pallas_call x0 -> x1, Pallas kernels: none -> 1.79 us  [per_device(): pl.pallas_call(finish, out_shape=(jax.ShapeDtypeStruct(query.shape, BF16)...]
    dynamic_slice x2 -> x0, local copies, waits for them, and re-layouts: 1.22 us -> none  [the longest x1 0.64 us: per_device(): pair_piece = lax.dynamic_slice(bias, (1, 32 * (dp % 4)), (2, 32))]
where the time goes in v2:
time: 96.7 us; the launch traced here: 96.5 us
  Pallas kernels  95.9 us (99%)
    pallas_call x1, Pallas kernels, per_device(): pl.pallas_call(kernel, out_shape=(jax.ShapeDtypeStruct(query.shape, BF16)...  94.1 us

profile of v2, /device:TPU:1, one launch (start us, length us, event | category | flops | bytes accessed | tf_op | source)
XLA Modules:
  0.0 96.5 jit_solution(14083884748150850677)
XLA Ops:
  0.6 94.1 %shard_map.101 = (bf16[2,64,4096]{2,1,0:T(8,128)(2,1)S(1)}, bf16[2,2,8,64,256]{4,3,2,1,0:T(8,128)(2,1)S(1)}, f32[8,128]{1,0:T(8,128)S(1)}) custom-call(bf16[2,64,4096]{2,1,0:T(8,128)(2,1)} %q_hbm.1, bf16[2,64,1024]{2,1,0:T(8,128)(2,1)} %k_hbm.1, bf16[2,64,1024]{2,1,0:T(8,128)(2,1)} %v_hbm.1, bf16[2,64,4096]{2,1,0:T(8,128)(2,1)} %o_hbm.1, ...), custom_call_target="tpu_custom_call" | custom-call | flops 6000000000 | bytes 8000000 | tf_op jit(solution)/shard_map/pallas_call | solution.py:343
  94.7 1.8 %shard_map.102 = (bf16[2,64,4096]{2,1,0:T(8,128)(2,1)}, bf16[2,64,1024]{2,1,0:T(8,128)(2,1)}, bf16[2,64,1024]{2,1,0:T(8,128)(2,1)}, f32[1,8]{1,0:T(1,128)}, f32[2,32]{1,0:T(2,128)}) custom-call(bf16[2,64,4096]{2,1,0:T(8,128)(2,1)S(1)} %get-tuple-element.8.dq, bf16[2,2,8,64,256]{4,3,2,1,0:T(8,128)(2,1)S(1)} %get-tuple-element.9.dkv, ...), custom_call_target="tpu_custom_call" | custom-call | tf_op jit(solution)/shard_map/pallas_call | solution.py:396

commit v3 on v2

--- a/solution.py
+++ b/solution.py
@@ -17,7 +17,7 @@
 TOK = 64
 DOCS = 2
 SLOTS = 8
-TILE = 4
+TILE = 8
 AHEAD = 5
 QW = GROUP * HD
 INV_ROOT = 1.0 / math.sqrt(HD)
@@ -198,7 +198,7 @@
         dv_acc[...] = jnp.zeros_like(dv_acc)
 
         def step(n, _):
-            h, part = lax.div(n, 2), lax.rem(n, 2)
+            h, part = lax.div(n, SLOTS // TILE), lax.rem(n, SLOTS // TILE)
             slots = pl.ds(part * TILE, TILE)
             q_cols = pl.ds(pl.multiple_of(h * HD, HD), HD)
             c_cols = pl.ds(pl.multiple_of(h * HD + QW, HD), HD)

time: 96.7 us -> 96 us (level)
  no operation moved by 1% of the time
where the time goes in v3:
time: 96 us; the launch traced here: 95.8 us
  Pallas kernels  95.2 us (99%)
    pallas_call x1, Pallas kernels, per_device(): pl.pallas_call(kernel, out_shape=(jax.ShapeDtypeStruct(query.shape, BF16)...  93.4 us

profile of v3, /device:TPU:1, one launch (start us, length us, event | category | flops | bytes accessed | tf_op | source)
XLA Modules:
  0.0 95.8 jit_solution(12012460937028707098)
XLA Ops:
  0.6 93.4 %shard_map.101 = (bf16[2,64,4096]{2,1,0:T(8,128)(2,1)S(1)}, bf16[2,2,8,64,256]{4,3,2,1,0:T(8,128)(2,1)S(1)}, f32[8,128]{1,0:T(8,128)S(1)}) custom-call(bf16[2,64,4096]{2,1,0:T(8,128)(2,1)} %q_hbm.1, bf16[2,64,1024]{2,1,0:T(8,128)(2,1)} %k_hbm.1, bf16[2,64,1024]{2,1,0:T(8,128)(2,1)} %v_hbm.1, bf16[2,64,4096]{2,1,0:T(8,128)(2,1)} %o_hbm.1, ...), custom_call_target="tpu_custom_call" | custom-call | flops 6000000000 | bytes 8000000 | tf_op jit(solution)/shard_map/pallas_call | solution.py:343
  94.0 1.8 %shard_map.102 = (bf16[2,64,4096]{2,1,0:T(8,128)(2,1)}, bf16[2,64,1024]{2,1,0:T(8,128)(2,1)}, bf16[2,64,1024]{2,1,0:T(8,128)(2,1)}, f32[1,8]{1,0:T(1,128)}, f32[2,32]{1,0:T(2,128)}) custom-call(bf16[2,64,4096]{2,1,0:T(8,128)(2,1)S(1)} %get-tuple-element.8.dq, bf16[2,2,8,64,256]{4,3,2,1,0:T(8,128)(2,1)S(1)} %get-tuple-element.9.dkv, ...), custom_call_target="tpu_custom_call" | custom-call | tf_op jit(solution)/shard_map/pallas_call | solution.py:396

commit v4 on v3

--- a/solution.py
+++ b/solution.py
@@ -39,9 +39,9 @@
     q_hbm, k_hbm, v_hbm, o_hbm, masked_hbm, bucket_hbm,
     dq_out, dkv_out, bias_out,
     q_in, k_in, v_in, o_in, masked, bucket, qc_stage, kv_stage, qc_buf, kv_buf, dq_stage, dkv_stage,
-    kt, dk_acc, dv_acc, bias_src, bias_all, msg, dp_buf, bias_sum, bias_in,
+    kt, dk_acc, dv_acc, bias_src, bias_all, q_src, q_all, msg, dp_buf, bias_sum, bias_in,
     in_sem, qc_send, qc_recv, kv_send, kv_recv, dq_send, dq_recv, dkv_send, dkv_recv,
-    bias_send, bias_recv, dp_sem, share_sem, go_sem,
+    bias_send, bias_recv, q_send, q_recv, dp_sem, share_sem, go_sem,
 ):
     me = lax.axis_index("ctx")
     dp = lax.axis_index("dp")
@@ -161,20 +161,20 @@
     def reduce_bias():
         for k in range(2):
             whole(bias_all.at[k], bias_recv.at[k])
-        first = lax.rem(y, 4) * 2
+        whole(q_all, q_recv)
         msg[...] = jnp.zeros_like(msg)
         for core in range(CORES):
             for b in range(2):
                 row = 2 * core + b
                 total = sum(
-                    bias_all[lax.div(y, 4), first + n, row : row + 1, :] for n in (0, 1, 8, 9)
+                    q_all[n, row : row + 1, :] for n in range(4)
                 )
                 for a in range(4 * b, 4 * b + 4):
                     msg[a, core : core + 1, :] = total
         for g in range(CHIPS):
             m, k = g % 4, g // 4
             msg[g, 2:4, :] = sum(
-                bias_all[k, 2 * m + n, GROUP : GROUP + 2, :] for n in (0, 1, 8, 9)
+                bias_all[k, 2 * m + n, :, :] for n in (0, 1, 8, 9)
             )
         pl.semaphore_wait(barrier, DP - 1)
         pltpu.make_async_copy(msg.at[lax.div(dp, 4)], dp_buf.at[dp], dp_sem.at[1]).start()
@@ -188,7 +188,6 @@
 
         lax.fori_loop(1, DP, send_msg, 0)
 
-    bias_src[...] = jnp.zeros_like(bias_src)
     for k in range(2):
         own = lax.rem(y, 4) + 4 * k
         whole(kv_buf.at[k], kv_recv.at[k])
@@ -218,14 +217,25 @@
             dk_acc[...] += nn(score_grad, q)
             grad = nn(kt[...], score_grad).T
             dq_stage[k, slots, :, q_cols] = grad.astype(BF16).reshape(TILE, TOK, HD)
-            bias_src[k, pl.ds(h, 1), :] += jnp.sum(grad, axis=0, keepdims=True)
+            q_src[k, pl.ds(h, 1), :] = jnp.sum(grad, axis=0, keepdims=True)
             return 0
 
         lax.fori_loop(0, GROUP * SLOTS // TILE, step, 0)
-        bias_src[k, GROUP : GROUP + 1, :] = jnp.sum(dk_acc[...], axis=0, keepdims=True)
-        bias_src[k, GROUP + 1 : GROUP + 2, :] = jnp.sum(dv_acc[...], axis=0, keepdims=True)
+        bias_src[k, 0:1, :] = jnp.sum(dk_acc[...], axis=0, keepdims=True)
+        bias_src[k, 1:2, :] = jnp.sum(dv_acc[...], axis=0, keepdims=True)
         dkv_stage[k, :, :, 0:HD] = dk_acc[...].astype(BF16).reshape(CTX, TOK, HD)
         dkv_stage[k, :, :, HD : 2 * HD] = dv_acc[...].astype(BF16).reshape(CTX, TOK, HD)
+
+        q_dst = q_all.at[2 * lax.div(y, 4) + c]
+        stays = jnp.logical_and(c == 1, lax.div(y, 4) == k)
+
+        @pl.when(stays)
+        def _():
+            pltpu.make_async_copy(q_src.at[k], q_dst, q_recv).start()
+
+        @pl.when(jnp.logical_not(stays))
+        def _():
+            remote(q_src.at[k], q_dst, q_send.at[k], q_recv, {"ctx": 2 * own + 1}).start()
 
         def send_bias(n, _):
             remote(
@@ -304,6 +314,12 @@
         whole(qc_buf.at[k, pl.ds(0, SLOTS - 1)], qc_send.at[k])
         whole(dkv_stage.at[k, pl.ds(0, CTX - 1)], dkv_send.at[k])
         whole(dq_stage.at[k, pl.ds(0, SLOTS - 1)], dq_send.at[k])
+
+    for k in range(2):
+
+        @pl.when(jnp.logical_not(jnp.logical_and(c == 1, lax.div(y, 4) == k)))
+        def _():
+            whole(q_src.at[k], q_send.at[k])
 
     @pl.when(c == 0)
     def _():
@@ -365,8 +381,10 @@
             pltpu.VMEM((HD, CTX * TOK), BF16),
             pltpu.VMEM((CTX * TOK, HD), F32),
             pltpu.VMEM((CTX * TOK, HD), F32),
-            pltpu.VMEM((2, 8, HD), F32),
-            pltpu.VMEM((2, CTX, 8, HD), F32),
+            pltpu.VMEM((2, 2, HD), F32),
+            pltpu.VMEM((2, CTX, 2, HD), F32),
+            pltpu.VMEM((2, GROUP, HD), F32),
+            pltpu.VMEM((4, GROUP, HD), F32),
             pltpu.VMEM((CHIPS, 8, HD), F32),
             pltpu.VMEM((DP, 8, HD), F32),
             pltpu.VMEM((8, HD), F32),
@@ -382,6 +400,8 @@
             dma,
             dma((2,)),
             dma((2,)),
+            dma((2,)),
+            dma,
             dma((2,)),
             dma((2,)),
             pltpu.SemaphoreType.REGULAR,

time: 96 us -> 95.8 us (level)
  no operation moved by 1% of the time
where the time goes in v4:
time: 95.8 us; the launch traced here: 95.6 us
  Pallas kernels  95 us (99%)
    pallas_call x1, Pallas kernels, per_device(): pl.pallas_call(kernel, out_shape=(jax.ShapeDtypeStruct(query.shape, BF16)...  93.2 us

profile of v4, /device:TPU:1, one launch (start us, length us, event | category | flops | bytes accessed | tf_op | source)
XLA Modules:
  0.0 95.6 jit_solution(18048825726277791831)
XLA Ops:
  0.6 93.2 %shard_map.101 = (bf16[2,64,4096]{2,1,0:T(8,128)(2,1)S(1)}, bf16[2,2,8,64,256]{4,3,2,1,0:T(8,128)(2,1)S(1)}, f32[8,128]{1,0:T(8,128)S(1)}) custom-call(bf16[2,64,4096]{2,1,0:T(8,128)(2,1)} %q_hbm.1, bf16[2,64,1024]{2,1,0:T(8,128)(2,1)} %k_hbm.1, bf16[2,64,1024]{2,1,0:T(8,128)(2,1)} %v_hbm.1, bf16[2,64,4096]{2,1,0:T(8,128)(2,1)} %o_hbm.1, ...), custom_call_target="tpu_custom_call" | custom-call | flops 6000000000 | bytes 8000000 | tf_op jit(solution)/shard_map/pallas_call | solution.py:359
  93.8 1.8 %shard_map.102 = (bf16[2,64,4096]{2,1,0:T(8,128)(2,1)}, bf16[2,64,1024]{2,1,0:T(8,128)(2,1)}, bf16[2,64,1024]{2,1,0:T(8,128)(2,1)}, f32[1,8]{1,0:T(1,128)}, f32[2,32]{1,0:T(2,128)}) custom-call(bf16[2,64,4096]{2,1,0:T(8,128)(2,1)S(1)} %get-tuple-element.8.dq, bf16[2,2,8,64,256]{4,3,2,1,0:T(8,128)(2,1)S(1)} %get-tuple-element.9.dkv, ...), custom_call_target="tpu_custom_call" | custom-call | tf_op jit(solution)/shard_map/pallas_call | solution.py:416
